TPU v7x, 512 devices: a whole 4x4x16 slice. The times are simulated.
512 devices in a mesh: dp: 4 (over x), row: 32 (over z, core), col: 4 (over y).
Axes of the slice: x: 4, y: 4, z: 16, core: 2. Of those that a mesh axis runs over, the one named last changes fastest.
Arguments:
- gate_grads: bfloat16 [4, 4096, 16384], P('dp', 'row', 'col'), may hold values from -1000 to 1000
- gate_rows: float32 [4096], P('row'), may hold values from 0.002 to 1
- gate_cols: float32 [16384], P('col'), may hold values from 0.002 to 1
- out_grads: bfloat16 [4, 16384, 4096], P('dp', 'row', 'col'), may hold values from -1000 to 1000
- out_rows: float32 [16384], P('row'), may hold values from 0.002 to 1
- out_cols: float32 [4096], P('col'), may hold values from 0.002 to 1
Outputs:
- gate_update: bfloat16 [4096, 16384], P('row', 'col')
- gate_rows_new: float32 [4096], P('row')
- gate_cols_new: float32 [16384], P('col')
- out_update: bfloat16 [16384, 4096], P('row', 'col')
- out_rows_new: float32 [16384], P('row')
- out_cols_new: float32 [4096], P('col')
All inputs are finite; a program needn't handle non-finite values.
Results may differ from a plain program's by a relative error of at most 0.015.
Values may be sent and summed in bfloat16 or wider, within the bound.
A program may use at most 64 MiB of HBM per device.

v0:
```python
import jax
import jax.numpy as jnp
from jax import lax
from jax.sharding import PartitionSpec as P

D = 4096
FF = 16384


beta_two = 0.8
tiny = 1e-30
clip_level = 1.0


def unit_of(summed, rows_new, cols_new):
    return summed / jnp.sqrt(rows_new[:, None] * cols_new[None, :])


def local(gate_grads, gate_rows, gate_cols, out_grads, out_rows, out_cols):
    replicas = lax.axis_size("dp")
    copies = replicas * lax.axis_size("col")
    rank = lax.axis_index("dp")
    gate_terms = gate_grads[0].astype(jnp.float32)
    out_terms = out_grads[0].astype(jnp.float32)
    gate_width = gate_terms.shape[1]
    out_width = out_terms.shape[1]
    gate_share = gate_width // replicas
    out_share = out_width // replicas
    gate_sum, out_sum = (
        lax.psum(gate_terms.astype(jnp.bfloat16), "dp").astype(jnp.float32),
        lax.psum(out_terms.astype(jnp.bfloat16), "dp").astype(jnp.float32),
    )
    gate_offset = rank * gate_share
    out_offset = rank * out_share
    gate_squares = gate_sum * gate_sum + tiny
    out_squares = out_sum * out_sum + tiny
    gate_row_part = jnp.sum(
        lax.dynamic_slice_in_dim(gate_squares, gate_offset, gate_share, 1), axis=1
    )
    out_row_part = jnp.sum(lax.dynamic_slice_in_dim(out_squares, out_offset, out_share, 1), axis=1)
    gate_col_part = jnp.sum(gate_squares, axis=0)
    out_col_part = jnp.sum(out_squares, axis=0)
    gate_row_tot, out_row_tot = lax.psum((gate_row_part, out_row_part), ("dp", "col"))
    gate_col_tot, out_col_tot = lax.psum((gate_col_part, out_col_part), "row")
    gate_rows_new = beta_two * gate_rows + (1.0 - beta_two) * (gate_row_tot / FF)
    gate_cols_new = beta_two * gate_cols + (1.0 - beta_two) * (gate_col_tot / D)
    out_rows_new = beta_two * out_rows + (1.0 - beta_two) * (out_row_tot / D)
    out_cols_new = beta_two * out_cols + (1.0 - beta_two) * (out_col_tot / FF)
    gate_unit = unit_of(gate_sum, gate_rows_new, gate_cols_new)
    out_unit = unit_of(out_sum, out_rows_new, out_cols_new)
    gate_piece = lax.dynamic_slice_in_dim(gate_unit, gate_offset, gate_share, 1)
    out_piece = lax.dynamic_slice_in_dim(out_unit, out_offset, out_share, 1)
    energies = (
        jnp.sum(gate_piece * gate_piece),
        jnp.sum(out_piece * out_piece),
        jnp.sum(gate_rows_new),
        jnp.sum(out_rows_new),
    )
    gate_energy, out_energy, gate_row_total, out_row_total = lax.psum(
        (energies[0], energies[1], energies[2], energies[3]), ("dp", "row", "col")
    )
    gate_mean = gate_row_total / (copies * D)
    out_mean = out_row_total / (copies * FF)
    gate_root = jnp.sqrt(gate_mean * gate_energy / (D * FF))
    out_root = jnp.sqrt(out_mean * out_energy / (D * FF))
    gate_factor = jnp.sqrt(gate_mean) / jnp.maximum(1.0, gate_root / clip_level)
    out_factor = jnp.sqrt(out_mean) / jnp.maximum(1.0, out_root / clip_level)
    gate_update = (gate_unit * gate_factor).astype(jnp.bfloat16)
    out_update = (out_unit * out_factor).astype(jnp.bfloat16)
    return (gate_update, gate_rows_new, gate_cols_new, out_update, out_rows_new, out_cols_new)


def solution(mesh):
    in_specs = (
        P("dp", "row", "col"),
        P("row"),
        P("col"),
        P("dp", "row", "col"),
        P("row"),
        P("col"),
    )
    out_specs = (P("row", "col"), P("row"), P("col"), P("row", "col"), P("row"), P("col"))
    return jax.shard_map(local, mesh=mesh, in_specs=in_specs, out_specs=out_specs, check_vma=False)
```

profile of v0, /device:TPU:1, one launch (start us, length us, event | category | flops | bytes accessed | tf_op | source)
XLA Modules:
  0.0 337.9 jit_solution(1096647130668392415)
XLA Ops:
  7.2 0.0 all-reduce.6.cloned.1.call-start
  7.2 0.7 all-reduce.6.cloned.1.call-update
  7.9 82.1 %all-reduce.6.cloned.1.call-done = (bf16[128,4096]{1,0:T(8,128)(2,1)}, bf16[512,1024]{1,0:T(8,128)(2,1)}) async-done(((bf16[128,4096]{1,0:T(8,128)(2,1)}, bf16[512,1024]{1,0:T(8,128)(2,1)}), (bf16[128,4096]{1,0:T(8,128)(2,1)}, bf16[512,1024]{1,0:T(8,128)(2,1)})) %all-reduce.6.cloned.1.call-update) | async-done | bytes 2097168 | tf_op jit(solution)/shard_map/psum | solution.py:30
  90.0 0.0 copy-start.1
  90.0 1.6 fusion.3
  91.7 0.0 copy-done.1
  91.7 0.0 copy-start.9
  91.7 0.0 copy-start.5
  91.7 0.0 copy-start
  91.7 0.4 fusion.2
  92.1 0.1 dynamic-slice_reduce_fusion.1
  92.2 0.0 copy-start.8
  92.2 0.0 copy-start.7
  92.3 0.2 dynamic-slice_reduce_fusion
  92.4 31.6 %all-reduce.2 = (f32[128]{0:T(128)S(1)}, f32[512]{0:T(512)S(1)}) all-reduce(f32[128]{0:T(128)S(1)} %dynamic-slice_reduce_fusion.1, f32[512]{0:T(512)S(1)} %dynamic-slice_reduce_fusion), channel_id=1, replica_groups=mesh['dp'=4,'row'=32,'col'=4] {'dp','col'}, use_global_device_ids=true, to_apply=%region_2.0 | all-reduce | flops 640 | bytes 5120 | tf_op jit(solution)/shard_map/psum | solution.py:43
  124.0 0.0 copy-done.9
  124.0 0.6 fusion.5
  124.6 0.0 copy-start.6
  124.6 95.3 %all-reduce.1 = (f32[4096]{0:T(1024)S(1)}, f32[1024]{0:T(1024)S(1)}) all-reduce(f32[4096]{0:T(1024)S(1)} %get-tuple-element.22, f32[1024]{0:T(1024)S(1)} %get-tuple-element.20), channel_id=1, replica_groups=mesh['dp'=4,'row'=32,'col'=4] {'row'}, use_global_device_ids=true, to_apply=%region_4.0 | all-reduce | flops 5120 | bytes 40960 | tf_op jit(solution)/shard_map/psum | solution.py:44
  219.9 0.0 copy-done.5
  219.9 0.0 copy-start.2
  219.9 0.0 copy-done
  219.9 0.4 convert_multiply_fusion.2
  220.3 0.7 multiply_reduce_fusion.1
  221.1 0.0 copy-done.8
  221.1 0.7 fusion.4
  221.8 0.0 copy-start.4
  221.8 0.0 copy-done.7
  221.8 0.0 copy-start.3
  221.8 0.3 convert_multiply_fusion
  222.1 0.8 multiply_reduce_fusion
  222.9 102.5 %all-reduce = (f32[]{:T(128)}, f32[]{:T(128)}, f32[]{:T(128)}, f32[]{:T(128)}) all-reduce(f32[]{:T(128)} %get-tuple-element.18, f32[]{:T(128)} %multiply_reduce_fusion.1, f32[]{:T(128)} %get-tuple-element.16, f32[]{:T(128)} %multiply_reduce_fusion), channel_id=1, replica_groups=mesh['dp'=4,'row'=32,'col'=4] {'dp','row','col'}, use_global_device_ids=true, to_apply=%region_6.0 | all-reduce | flops 4 | bytes 32 | tf_op jit(solution)/shard_map/psum | solution.py:59
  326.9 0.0 copy-done.6
  326.9 0.0 copy-done.2
  326.9 1.4 multiply_convert_fusion.1
  329.6 0.0 copy-done.4
  329.6 0.0 copy-done.3
  329.6 1.4 multiply_convert_fusion
  (2 shorter events, 0.0 us)
Async XLA Ops:
  7.2 82.9 %all-reduce.6.cloned.1.call-start = ((), (), s32[]{:S(2)}) async-start(), calls=%async_computation | async-start | bytes 4194304 | tf_op jit(solution)/shard_map/psum | solution.py:30
  90.0 1.7 copy-start.1
  91.7 32.3 %copy-start.9 = (f32[128]{0:T(128)S(1)}, f32[128]{0:T(128)}, u32[]{:S(2)}) copy-start(f32[128]{0:T(128)} %param.7) | copy-start | bytes 1540
  91.7 128.2 %copy-start.5 = (f32[4096]{0:T(1024)S(1)}, f32[4096]{0:T(1024)}, u32[]{:S(2)}) copy-start(f32[4096]{0:T(1024)} %param.8) | copy-start | bytes 49156
  91.7 128.2 %copy-start = (bf16[128,4096]{1,0:T(8,128)(2,1)S(1)}, bf16[128,4096]{1,0:T(8,128)(2,1)}, u32[]{:S(2)}) copy-start(bf16[128,4096]{1,0:T(8,128)(2,1)} %get-tuple-element.14) | copy-start | bytes 3145732
  92.2 128.8 %copy-start.8 = (f32[512]{0:T(512)S(1)}, f32[512]{0:T(512)}, u32[]{:S(2)}) copy-start(f32[512]{0:T(512)} %param.10) | copy-start | bytes 6148
  92.2 129.5 %copy-start.7 = (f32[1024]{0:T(1024)S(1)}, f32[1024]{0:T(1024)}, u32[]{:S(2)}) copy-start(f32[1024]{0:T(1024)} %param.11) | copy-start | bytes 12292
  124.6 202.3 %copy-start.6 = (f32[128]{0:T(128)}, f32[128]{0:T(128)S(1)}, u32[]{:S(2)}) copy-start(f32[128]{0:T(128)S(1)} %get-tuple-element.19) | copy-start | bytes 1540
  219.9 107.0 %copy-start.2 = (f32[4096]{0:T(1024)}, f32[4096]{0:T(1024)S(1)}, u32[]{:S(2)}) copy-start(f32[4096]{0:T(1024)S(1)} %multiply_add_fusion) | copy-start | bytes 49156
  221.8 107.9 %copy-start.4 = (f32[512]{0:T(512)}, f32[512]{0:T(512)S(1)}, u32[]{:S(2)}) copy-start(f32[512]{0:T(512)S(1)} %get-tuple-element.17) | copy-start | bytes 6148
  221.8 107.9 %copy-start.3 = (f32[1024]{0:T(1024)}, f32[1024]{0:T(1024)S(1)}, u32[]{:S(2)}) copy-start(f32[1024]{0:T(1024)S(1)} %multiply_add_fusion.1) | copy-start | bytes 12292
Sparse Core Ops, SparseCore 0:
  10.4 79.5 all-reduce.5
where the time goes:
time: 338 us
  blocking collectives  229 us (68%)
  waiting for transfers between devices  82.8 us (24%)
  between operations  16.9 us (5%)
  other arithmetic  8.71 us (3%)
    psum x1, blocking collectives, local(): lax.psum((energies[0], energies[1], energies[2], energies[3]), ('dp', 'ro...  103 us
    psum x1, blocking collectives, local(): gate_col_tot, out_col_tot = lax.psum((gate_col_part, out_col_part), 'row')  95.3 us
    psum x1, waiting for transfers between devices, local(): lax.psum(gate_terms.astype(jnp.bfloat16), 'dp').astype(jnp.float32)  82.1 us
    psum x1, blocking collectives, local(): lax.psum((gate_row_part, out_row_part), ('dp', 'col'))  31.6 us
  transfers between devices with their start and end apart: 1, of which 1 were waited for; matrix products, arithmetic and copies ran while one was open for 0% of the time, Pallas kernels for 0%

commit v1 on v0

v1 whole, which is shorter than its diff:
```python
import functools

import jax
import jax.numpy as jnp
from jax import lax
from jax.experimental import pallas as pl
from jax.experimental.pallas import tpu as pltpu
from jax.sharding import PartitionSpec as P

D = 4096
FF = 16384
KEEP = 0.8
TINY = 1e-30
MESH = pl.DeviceIdType.MESH
F32 = jnp.float32
BF16 = jnp.bfloat16


class Mat:
    def __init__(self, rows, width, m, n, first_row):
        self.rows, self.width, self.m, self.n, self.first_row = rows, width, m, n, first_row
        self.chunk = width // 4
        self.half = rows // 2
        self.tiles = self.chunk // 128


GATE = Mat(128, 4096, D, FF, 0)
OUT = Mat(512, 1024, FF, D, 128)
MATS = (GATE, OUT)


def cols_of(mat, k):
    return pl.ds(pl.multiple_of(k * mat.chunk, 128), mat.chunk)


def half_of(mat, h):
    return pl.ds(h * mat.half, mat.half)


def rcopy(src, dst, send, recv, dev):
    return pltpu.make_async_remote_copy(
        src_ref=src, dst_ref=dst, send_sem=send, recv_sem=recv, device_id=dev, device_id_type=MESH
    )


def kernel(
    zs,
    gate_in, gate_rows, gate_cols, out_in, out_rows, out_cols,
    gate_up, gate_rows_new, gate_cols_new, out_up, out_rows_new, out_cols_new,
    own_g, own_o, tr_g, tr_o, st_g, st_o, fr_g, fr_o, full_g, full_o, res_g, res_o,
    sq_g, sq_o, lanes, rmat, rows_buf, q_mine, q_sib, q_z, w_mine, w_sib, w_z, e_buf, cf_g, cf_o,
    load_sem, store_sem, rs_send, rs_recv, ag_send, ag_recv,
    s1_send, s1_recv, core_send, core_recv, z_send, z_recv, s3_send, s3_recv,
):
    x, r, y = lax.axis_index("dp"), lax.axis_index("row"), lax.axis_index("col")
    z, core = r // 2, r % 2
    right, left, over = (x + 1) % 4, (x + 3) % 4, (x + 2) % 4
    dev = ((right, r, y), (left, r, y))
    sibling = (x, z * 2 + (1 - core), y)
    ins, own, tr, st, fr, full, res = (
        (gate_in, out_in), (own_g, own_o), (tr_g, tr_o), (st_g, st_o), (fr_g, fr_o), (full_g, full_o), (res_g, res_o),
    )

    loads = [
        pltpu.make_async_copy(ins[i].at[0], own[i], load_sem.at[i]) for i in range(2)
    ]
    for load in loads:
        load.start()

    xy_partners = [((x + i) % 4, (y + j) % 4) for i in range(4) for j in range(4) if i or j]
    z_partners = [(z + k) % zs for k in range(1, zs)]
    barrier = pltpu.get_barrier_semaphore()
    greet = (
        [(a, r, b) for a, b in xy_partners]
        + [(a, z * 2 + (1 - core), b) for a, b in xy_partners]
        + [sibling]
        + [(x, k * 2 + core, y) for k in z_partners]
    )
    for who in greet:
        pl.semaphore_signal(barrier, inc=1, device_id=who, device_id_type=MESH)
    q_mine[...] = jnp.zeros_like(q_mine)
    w_mine[...] = jnp.zeros_like(w_mine)
    for load in loads:
        load.wait()
    pl.semaphore_wait(barrier, len(greet))

    sends = []

    def go(copy):
        copy.start()
        sends.append(copy)

    def rs_transit(i, d):
        return rcopy(
            own[i].at[half_of(MATS[i], d), cols_of(MATS[i], over)], tr[i].at[d],
            rs_send.at[i, d, 0], rs_recv.at[i, d, 0], dev[d],
        )

    def rs_alone(i, d):
        to = (right, left)[d]
        return rcopy(
            own[i].at[half_of(MATS[i], 1 - d), cols_of(MATS[i], to)], fr[i].at[d, half_of(MATS[i], 1 - d)],
            rs_send.at[i, d, 1], rs_recv.at[i, d, 1], dev[d],
        )

    def rs_sum(i, d):
        return rcopy(
            st[i].at[d], fr[i].at[d, half_of(MATS[i], d)],
            rs_send.at[i, d, 2], rs_recv.at[i, d, 2], dev[d],
        )

    for make in (rs_transit, rs_alone):
        for i in range(2):
            for d in range(2):
                go(make(i, d))
    for i in range(2):
        mat = MATS[i]
        for d in range(2):
            to = (right, left)[d]
            rs_transit(i, d).wait_recv()
            step = 16384 // mat.chunk

            def add(n, _, i=i, d=d, to=to, mat=mat, step=step):
                rows = pl.ds(pl.multiple_of(n * step, 16), step)
                mine = own[i][pl.ds(pl.multiple_of(d * mat.half + n * step, 16), step), cols_of(mat, to)]
                st[i][d, rows, :] = (mine.astype(F32) + tr[i][d, rows, :].astype(F32)).astype(BF16)
                return 0

            lax.fori_loop(0, mat.half // step, add, 0)
            go(rs_sum(i, d))

    me_xy = x * 4 + y
    for i in range(2):
        mat = MATS[i]
        sq = (sq_g, sq_o)[i]
        for d in range(2):
            rs_alone(i, d).wait_recv()
            rs_sum(i, d).wait_recv()
        step = 16384 // mat.chunk

        def total(n, acc, i=i, mat=mat, sq=sq, step=step):
            rows = pl.ds(pl.multiple_of(n * step, 16), step)
            s = own[i][rows, cols_of(mat, x)].astype(F32) + fr[i][0, rows, :].astype(F32) + fr[i][1, rows, :].astype(F32)
            full[i][rows, cols_of(mat, x)] = s.astype(BF16)
            s = s * s
            sq[rows, :] = s
            by_lane = s[:, 0:128]
            for t in range(1, mat.tiles):
                by_lane = by_lane + s[:, t * 128 : (t + 1) * 128]
            lanes[pl.ds(pl.multiple_of(mat.first_row + n * step, 8), step), :] = by_lane
            for k in range(step // 8):
                acc = acc + s[k * 8 : (k + 1) * 8, :]
            return acc

        acc = lax.fori_loop(0, mat.rows // step, total, jnp.zeros((8, mat.chunk), F32))
        col = jnp.sum(acc, axis=0, keepdims=True)
        for h in range(2):
            for t in range(mat.tiles // 2):
                k = h * (mat.tiles // 2) + t
                at = t if i == 0 else 4
                q_mine[h, at : at + 1, :] = col[:, k * 128 : (k + 1) * 128]
    for b in range(5):
        block = lanes[b * 128 : (b + 1) * 128, :].T
        rows_buf[me_xy, b : b + 1, :] = jnp.sum(block, axis=0, keepdims=True)

    def s1(a, b, peer):
        return rcopy(
            rows_buf.at[me_xy if peer is None else peer, pl.ds(0, 5)], rows_buf.at[me_xy if peer is None else peer, pl.ds(0, 5)],
            s1_send.at[a * 4 + b], s1_recv.at[me_xy if peer is None else peer], (a, r, b),
        )

    for a, b in xy_partners:
        go(s1(a, b, None))

    def to_core(buf, got, j):
        return rcopy(buf.at[1 - core], got, core_send.at[j], core_recv.at[j], sibling)

    go(to_core(q_mine, q_sib, 0))

    def ag_own(i, d, p):
        h = d if p == 0 else 1 - d
        ref = full[i].at[half_of(MATS[i], h), cols_of(MATS[i], x)]
        return rcopy(ref, ref, ag_send.at[i, d, p], ag_recv.at[i, d, p], dev[d])

    def ag_landed(i, d, p):
        h = d if p != 1 else 1 - d
        k = over if p == 2 else (left, right)[d]
        ref = full[i].at[half_of(MATS[i], h), cols_of(MATS[i], k)]
        return rcopy(ref, ref, ag_send.at[i, d, p], ag_recv.at[i, d, p], dev[d])

    def ag_forward(i, d):
        ref = full[i].at[half_of(MATS[i], d), cols_of(MATS[i], (left, right)[d])]
        return rcopy(ref, ref, ag_send.at[i, d, 2], ag_recv.at[i, d, 2], dev[d])

    for p in range(2):
        for i in range(2):
            for d in range(2):
                go(ag_own(i, d, p))

    def to_z(buf, j, k, peer):
        slot = z if peer is None else peer
        return rcopy(
            buf.at[slot], buf.at[slot], z_send.at[j, k], z_recv.at[j, slot], (x, k * 2 + core, y)
        )

    to_core(q_mine, q_sib, 0).wait_recv()
    q_z[z] = q_mine[core] + q_sib[...]
    for k in z_partners:
        go(to_z(q_z, 0, k, None))

    for a, b in xy_partners:
        s1(a, b, a * 4 + b).wait_recv()
    row_sum = rows_buf[0, 0:5, :]
    for k in range(1, 16):
        row_sum = row_sum + rows_buf[k, 0:5, :]
    g_rows = KEEP * gate_rows[...] + (1.0 - KEEP) * (row_sum[0:1] * (1.0 / FF) + TINY)
    o_rows = KEEP * out_rows[...] + (1.0 - KEEP) * (row_sum[1:5] * (1.0 / D) + TINY)
    gate_rows_new[...] = g_rows
    out_rows_new[...] = o_rows
    for b in range(5):
        one = g_rows if b == 0 else o_rows[b - 1 : b]
        rmat[b * 128 : (b + 1) * 128, :] = jnp.broadcast_to(lax.rsqrt(one), (128, 128)).T

    for i in range(2):
        mat = MATS[i]
        sq = (sq_g, sq_o)[i]
        step = 16384 // mat.chunk

        def weigh(n, acc, mat=mat, sq=sq, step=step):
            f = rmat[pl.ds(pl.multiple_of(mat.first_row + n * step, 8), step), :]
            f = f * f
            out = []
            for t in range(mat.tiles):
                p = sq[pl.ds(pl.multiple_of(n * step, 8), step), t * 128 : (t + 1) * 128] * f
                a = acc[t]
                for k in range(step // 8):
                    a = a + p[k * 8 : (k + 1) * 8, :]
                out.append(a)
            return tuple(out)

        acc = lax.fori_loop(0, mat.rows // step, weigh, tuple(jnp.zeros((8, 128), F32) for _ in range(mat.tiles)))
        for h in range(2):
            for t in range(mat.tiles // 2):
                at = t if i == 0 else 4
                w_mine[h, at : at + 1, :] = jnp.sum(acc[h * (mat.tiles // 2) + t], axis=0, keepdims=True)
    for h in range(2):
        w_mine[h, 5:6, :] = g_rows
        w_mine[h, 6:7, :] = jnp.sum(o_rows, axis=0, keepdims=True)
    go(to_core(w_mine, w_sib, 1))
    to_core(w_mine, w_sib, 1).wait_recv()
    w_z[z] = w_mine[core] + w_sib[...]
    for k in z_partners:
        go(to_z(w_z, 1, k, None))

    for i in range(2):
        for d in range(2):
            ag_landed(i, d, 0).wait_recv()
            go(ag_forward(i, d))

    for k in z_partners:
        to_z(q_z, 0, k, k).wait_recv()
    q = q_z[0]
    for k in range(1, zs):
        q = q + q_z[k]
    old_g = gate_cols[pl.ds(pl.multiple_of(x * 8 + core * 4, 4), 4), :]
    old_o = out_cols[pl.ds(x * 2 + core, 1), :]
    c_g = KEEP * old_g + (1.0 - KEEP) * (q[0:4] * (1.0 / D) + TINY)
    c_o = KEEP * old_o + (1.0 - KEEP) * (q[4:5] * (1.0 / FF) + TINY)
    for k in z_partners:
        to_z(w_z, 1, k, k).wait_recv()
    w = w_z[0]
    for k in range(1, zs):
        w = w + w_z[k]
    me_e = (x * 4 + y) * 2 + core
    e_buf[me_e, 0:4, :] = c_g
    e_buf[me_e, 4:5, :] = c_o
    e_buf[me_e, 5:6, :] = jnp.sum(w[0:4] / c_g, axis=0, keepdims=True)
    e_buf[me_e, 6:7, :] = w[4:5] / c_o
    e_buf[me_e, 7:8, :] = jnp.zeros((1, 128), F32)

    def s3(a, b, h, peer):
        slot = me_e if peer is None else peer
        return rcopy(
            e_buf.at[slot], e_buf.at[slot], s3_send.at[(a * 4 + b) * 2 + h], s3_recv.at[slot], (a, z * 2 + h, b)
        )

    e_partners = [(x, y, 1 - core)] + [(a, b, h) for a, b in xy_partners for h in (core, 1 - core)]
    for a, b, h in e_partners:
        go(s3(a, b, h, None))

    row_total = (jnp.sum(w[5:6]), jnp.sum(w[6:7]))
    for i in range(2):
        for d in range(2):
            for p in (1, 2):
                ag_landed(i, d, p).wait_recv()
    for a, b, h in e_partners:
        s3(a, b, h, (a * 4 + b) * 2 + h).wait_recv()
    e = e_buf[0, 5:7, :]
    for k in range(1, 32):
        e = e + e_buf[k, 5:7, :]
    factors = []
    for i in range(2):
        mean = row_total[i] * (1.0 / MATS[i].m)
        energy = jnp.sum(e[i : i + 1])
        mean = jnp.full((1, 128), mean, F32)
        root = jnp.sqrt(mean * (energy * (1.0 / (D * FF))))
        factors.append(jnp.sqrt(mean) / jnp.maximum(1.0, root))
    for k in range(4):
        for h in range(2):
            slot = (k * 4 + y) * 2 + h
            gate_cols_new[8 * k + 4 * h : 8 * k + 4 * h + 4, :] = e_buf[slot, 0:4, :]
            out_cols_new[2 * k + h : 2 * k + h + 1, :] = e_buf[slot, 4:5, :]
    cf_g[...] = lax.rsqrt(gate_cols_new[...]) * factors[0]
    cf_o[...] = lax.rsqrt(out_cols_new[...]) * factors[1]

    stores = []
    for k in range(4):

        def scale(t, _, k=k):
            cols = pl.ds(pl.multiple_of((k * 8 + t) * 128, 128), 128)
            res_g[:, cols] = (full_g[:, cols].astype(F32) * rmat[0:128, :] * cf_g[pl.ds(k * 8 + t, 1), :]).astype(BF16)
            return 0

        lax.fori_loop(0, 8, scale, 0)
        part = res_g.at[:, pl.ds(k * 1024, 1024)]
        stores.append(pltpu.make_async_copy(part, gate_up.at[:, pl.ds(k * 1024, 1024)], store_sem.at[k]))
        stores[-1].start()
    for k in range(4):

        def scale(t, _, k=k):
            cols = pl.ds(pl.multiple_of(t * 128, 128), 128)
            rows = pl.ds(k * 128, 128)
            res_o[rows, cols] = (full_o[rows, cols].astype(F32) * rmat[(k + 1) * 128 : (k + 2) * 128, :] * cf_o[pl.ds(t, 1), :]).astype(BF16)
            return 0

        lax.fori_loop(0, 8, scale, 0)
        part = res_o.at[pl.ds(k * 128, 128)]
        stores.append(pltpu.make_async_copy(part, out_up.at[pl.ds(k * 128, 128)], store_sem.at[4 + k]))
        stores[-1].start()
    for copy in sends:
        copy.wait_send()
    for store in stores:
        store.wait()


def local(zs, gate_grads, gate_rows, gate_cols, out_grads, out_rows, out_cols):
    vmem, hbm = pl.BlockSpec(memory_space=pltpu.VMEM), pl.BlockSpec(memory_space=pl.ANY)
    dma, buf = pltpu.SemaphoreType.DMA, pltpu.VMEM
    tile = (8, 128)
    outs = pl.pallas_call(
        functools.partial(kernel, zs),
        out_shape=(
            jax.ShapeDtypeStruct((128, 4096), BF16),
            jax.ShapeDtypeStruct((1, 128), F32),
            jax.ShapeDtypeStruct((32, 128), F32),
            jax.ShapeDtypeStruct((512, 1024), BF16),
            jax.ShapeDtypeStruct((4, 128), F32),
            jax.ShapeDtypeStruct((8, 128), F32),
        ),
        in_specs=[hbm, vmem, vmem, hbm, vmem, vmem],
        out_specs=(hbm, vmem, vmem, hbm, vmem, vmem),
        scratch_shapes=[
            buf((128, 4096), BF16), buf((512, 1024), BF16),
            buf((2, 64, 1024), BF16), buf((2, 256, 256), BF16),
            buf((2, 64, 1024), BF16), buf((2, 256, 256), BF16),
            buf((2, 128, 1024), BF16), buf((2, 512, 256), BF16),
            buf((128, 4096), BF16), buf((512, 1024), BF16),
            buf((128, 4096), BF16), buf((512, 1024), BF16),
            buf((128, 1024), F32), buf((512, 256), F32),
            buf((640, 128), F32), buf((640, 128), F32),
            buf((16, *tile), F32),
            buf((2, *tile), F32), buf(tile, F32), buf((zs, *tile), F32),
            buf((2, *tile), F32), buf(tile, F32), buf((zs, *tile), F32),
            buf((32, *tile), F32), buf((32, 128), F32), buf(tile, F32),
            dma((2,)), dma((8,)), dma((2, 2, 3)), dma((2, 2, 3)), dma((2, 2, 3)), dma((2, 2, 3)),
            dma((16,)), dma((16,)), dma((2,)), dma((2,)), dma((2, zs)), dma((2, zs)), dma((32,)), dma((32,)),
        ],
        compiler_params=pltpu.CompilerParams(collective_id=0, has_side_effects=True, vmem_limit_bytes=48 << 20),
    )(
        gate_grads, gate_rows.reshape(1, 128), gate_cols.reshape(32, 128),
        out_grads, out_rows.reshape(4, 128), out_cols.reshape(8, 128),
    )
    gate_up, gate_r, gate_c, out_up, out_r, out_c = outs
    return gate_up, gate_r.reshape(128), gate_c.reshape(4096), out_up, out_r.reshape(512), out_c.reshape(1024)


def solution(mesh):
    in_specs = (P("dp", "row", "col"), P("row"), P("col"), P("dp", "row", "col"), P("row"), P("col"))
    out_specs = (P("row", "col"), P("row"), P("col"), P("row", "col"), P("row"), P("col"))
    return jax.shard_map(
        functools.partial(local, mesh.shape["row"] // 2), mesh=mesh, in_specs=in_specs, out_specs=out_specs, check_vma=False
    )
```

time: 338 us -> 71.7 us (0.21)
  blocking collectives: 229 us -> 0 us
  waiting for transfers between devices: 82.8 us -> 0 us
  Pallas kernels: 0 us -> 62.6 us
  between operations: 16.9 us -> 0.67 us
  other arithmetic: 8.71 us -> 0 us
  local copies, waits for them, and re-layouts: 0.05 us -> 8.07 us
    psum x3 -> x0, blocking collectives: 229 us -> none  [the longest x1 103 us: local(): lax.psum((energies[0], energies[1], energies[2], energies[3]), ('dp', 'ro...]
    psum x1 -> x0, waiting for transfers between devices: 82.1 us -> none  [local(): lax.psum(gate_terms.astype(jnp.bfloat16), 'dp').astype(jnp.float32)]
    pallas_call x0 -> x1, Pallas kernels: none -> 62.6 us  [local(): pl.pallas_call(functools.partial(kernel, zs), out_shape=(jax.ShapeDtypeSt...]
    unnamed x20 -> x18, local copies, waits for them, and re-layouts: 0.05 us -> 8.07 us
    reduce_sum x8 -> x0, other arithmetic: 5.09 us -> none  [the longest x1 1.64 us: local(): gate_col_part = jnp.sum(gate_squares, axis=0)]
  transfers between devices with their start and end apart: 1 -> 0, of which waited for: 1 -> 0; matrix products, arithmetic and copies ran while one was open for 0% -> 0% of each run, Pallas kernels for 0% -> 0%
where the time goes in v1:
time: 71.7 us; the launch traced here: 71.4 us
  Pallas kernels  62.6 us (87%)
  local copies, waits for them, and re-layouts  8.07 us (11%)
    pallas_call x1, Pallas kernels, local(): pl.pallas_call(functools.partial(kernel, zs), out_shape=(jax.ShapeDtypeSt...  62.6 us
    unnamed x18, local copies, waits for them, and re-layouts  8.07 us

profile of v1, /device:TPU:1, one launch (start us, length us, event | category | flops | bytes accessed | tf_op | source)
XLA Modules:
  0.0 71.4 jit_solution(18440505093443529614)
XLA Ops:
  0.6 0.0 copy-start.3
  0.6 0.0 copy-start.4
  0.7 0.0 copy-start.5
  0.7 0.7 copy-done.3
  1.3 0.0 copy-done.4
  1.3 0.0 copy-done.5
  1.3 0.0 copy-start
  1.3 1.2 %copy-done = bf16[1,128,4096]{2,1,0:T(8,128)(2,1)S(1)} copy-done((bf16[1,128,4096]{2,1,0:T(8,128)(2,1)S(1)}, bf16[1,128,4096]{2,1,0:T(8,128)(2,1)}, u32[]{:S(2)}) %copy-start) | copy-done | bytes 1048600
  2.6 0.0 copy-start.1
  2.6 1.2 %copy-done.1 = bf16[1,512,1024]{2,1,0:T(8,128)(2,1)S(1)} copy-done((bf16[1,512,1024]{2,1,0:T(8,128)(2,1)S(1)}, bf16[1,512,1024]{2,1,0:T(8,128)(2,1)}, u32[]{:S(2)}) %copy-start.1) | copy-done | bytes 1048600
  3.8 0.0 copy-start.2
  3.8 0.7 %copy-done.2 = f32[4096]{0:T(1024)S(1)} copy-done((f32[4096]{0:T(1024)S(1)}, f32[4096]{0:T(1024)}, u32[]{:S(2)}) %copy-start.2) | copy-done | bytes 16408
  4.5 62.6 %shard_map.109 = (bf16[128,4096]{1,0:T(8,128)(2,1)S(1)}, f32[1,128]{1,0:T(1,128)S(1)}, f32[32,128]{1,0:T(8,128)S(1)}, bf16[512,1024]{1,0:T(8,128)(2,1)S(1)}, f32[4,128]{1,0:T(4,128)S(1)}, /*index=5*/f32[8,128]{1,0:T(8,128)S(1)}) custom-call(bf16[1,128,4096]{2,1,0:T(8,128)(2,1)S(1)} %copy-done, f32[1,128]{1,0:T(1,128)S(1)} %bitcast.14, ...), custom_call_target="tpu_custom_call" | custom-call | tf_op jit(solution)/shard_map/pallas_call | solution.py:350
  67.2 1.0 %copy.18 = bf16[128,4096]{1,0:T(8,128)(2,1)} copy(bf16[128,4096]{1,0:T(8,128)(2,1)S(1)} %get-tuple-element.24) | data formatting | bytes 2097152
  68.1 0.5 copy.19
  68.6 0.6 copy.20
  69.2 1.0 %copy.21 = bf16[512,1024]{1,0:T(8,128)(2,1)} copy(bf16[512,1024]{1,0:T(8,128)(2,1)S(1)} %get-tuple-element.27) | data formatting | bytes 2097152
  70.2 0.6 copy.22
  70.8 0.6 copy.23
Async XLA Ops:
  0.6 0.7 copy-start.3
  0.6 0.7 copy-start.4
  0.7 0.7 copy-start.5
  1.3 1.2 %copy-start = (bf16[1,128,4096]{2,1,0:T(8,128)(2,1)S(1)}, bf16[1,128,4096]{2,1,0:T(8,128)(2,1)}, u32[]{:S(2)}) copy-start(bf16[1,128,4096]{2,1,0:T(8,128)(2,1)} %gate_in.1) | copy-start | bytes 3145732
  2.6 1.2 %copy-start.1 = (bf16[1,512,1024]{2,1,0:T(8,128)(2,1)S(1)}, bf16[1,512,1024]{2,1,0:T(8,128)(2,1)}, u32[]{:S(2)}) copy-start(bf16[1,512,1024]{2,1,0:T(8,128)(2,1)} %out_in.1) | copy-start | bytes 3145732
  3.8 0.7 %copy-start.2 = (f32[4096]{0:T(1024)S(1)}, f32[4096]{0:T(1024)}, u32[]{:S(2)}) copy-start(f32[4096]{0:T(1024)} %param.8) | copy-start | bytes 49156

commit v2 on v1

--- a/solution.py
+++ b/solution.py
@@ -45,11 +45,12 @@
 
 def kernel(
     zs,
-    gate_in, gate_rows, gate_cols, out_in, out_rows, out_cols,
-    gate_up, gate_rows_new, gate_cols_new, out_up, out_rows_new, out_cols_new,
-    own_g, own_o, tr_g, tr_o, st_g, st_o, fr_g, fr_o, full_g, full_o, res_g, res_o,
-    sq_g, sq_o, lanes, rmat, rows_buf, q_mine, q_sib, q_z, w_mine, w_sib, w_z, e_buf, cf_g, cf_o,
-    load_sem, store_sem, rs_send, rs_recv, ag_send, ag_recv,
+    gate_in, gate_rows_in, gate_cols_in, out_in, out_rows_in, out_cols_in,
+    full_g, full_o, rmat, cf_g, cf_o, gate_rows_new, gate_cols_new, out_rows_new, out_cols_new,
+    gate_rows, gate_cols, out_rows, out_cols,
+    own_g, own_o, tr_g, tr_o, st_g, st_o, fr_g, fr_o,
+    sq_g, sq_o, lanes, rows_buf, q_mine, q_sib, q_z, w_mine, w_sib, w_z, e_buf,
+    token, load_sem, rs_send, rs_recv, ag_send, ag_recv,
     s1_send, s1_recv, core_send, core_recv, z_send, z_recv, s3_send, s3_recv,
 ):
     x, r, y = lax.axis_index("dp"), lax.axis_index("row"), lax.axis_index("col")
@@ -57,32 +58,42 @@
     right, left, over = (x + 1) % 4, (x + 3) % 4, (x + 2) % 4
     dev = ((right, r, y), (left, r, y))
     sibling = (x, z * 2 + (1 - core), y)
-    ins, own, tr, st, fr, full, res = (
-        (gate_in, out_in), (own_g, own_o), (tr_g, tr_o), (st_g, st_o), (fr_g, fr_o), (full_g, full_o), (res_g, res_o),
-    )
+    own, tr, st, fr, full = (own_g, own_o), (tr_g, tr_o), (st_g, st_o), (fr_g, fr_o), (full_g, full_o)
 
     loads = [
-        pltpu.make_async_copy(ins[i].at[0], own[i], load_sem.at[i]) for i in range(2)
+        pltpu.make_async_copy(src, dst, load_sem.at[i])
+        for i, (src, dst) in enumerate(
+            (
+                (gate_in.at[0], own_g), (out_in.at[0], own_o),
+                (gate_rows_in, gate_rows), (gate_cols_in, gate_cols), (out_rows_in, out_rows), (out_cols_in, out_cols),
+            )
+        )
     ]
     for load in loads:
         load.start()
 
     xy_partners = [((x + i) % 4, (y + j) % 4) for i in range(4) for j in range(4) if i or j]
     z_partners = [(z + k) % zs for k in range(1, zs)]
+    along_z = lambda k: (x, ((z + k + zs) % zs) * 2 + core, y)
+    across_x, across_y = (over, r, y), (x, r, (y + 2) % 4)
+    nearest = [dev[0], dev[1], (x, r, (y + 1) % 4), (x, r, (y + 3) % 4), along_z(1), along_z(-1), sibling]
+    rounds = (nearest, [across_x, across_y, along_z(2), along_z(-2), sibling], [along_z(4), along_z(-4), across_x])
+
+    def tell(k):
+        for who in rounds[k]:
+            pl.semaphore_signal(token.at[k], inc=1, device_id=who, device_id_type=MESH)
+
+    def hear(k):
+        pl.semaphore_wait(token.at[k], len(rounds[k]))
+
     barrier = pltpu.get_barrier_semaphore()
-    greet = (
-        [(a, r, b) for a, b in xy_partners]
-        + [(a, z * 2 + (1 - core), b) for a, b in xy_partners]
-        + [sibling]
-        + [(x, k * 2 + core, y) for k in z_partners]
-    )
-    for who in greet:
+    for who in nearest:
         pl.semaphore_signal(barrier, inc=1, device_id=who, device_id_type=MESH)
     q_mine[...] = jnp.zeros_like(q_mine)
     w_mine[...] = jnp.zeros_like(w_mine)
     for load in loads:
         load.wait()
-    pl.semaphore_wait(barrier, len(greet))
+    pl.semaphore_wait(barrier, len(nearest))
 
     sends = []
 
@@ -113,6 +124,7 @@
         for i in range(2):
             for d in range(2):
                 go(make(i, d))
+    tell(0)
     for i in range(2):
         mat = MATS[i]
         for d in range(2):
@@ -128,6 +140,23 @@
 
             lax.fori_loop(0, mat.half // step, add, 0)
             go(rs_sum(i, d))
+        hear(i)
+        tell(i + 1)
+
+    def ag_own(i, d, p):
+        h = d if p == 0 else 1 - d
+        ref = full[i].at[half_of(MATS[i], h), cols_of(MATS[i], x)]
+        return rcopy(ref, ref, ag_send.at[i, d, p], ag_recv.at[i, d, p], dev[d])
+
+    def ag_landed(i, d, p):
+        h = d if p != 1 else 1 - d
+        k = over if p == 2 else (left, right)[d]
+        ref = full[i].at[half_of(MATS[i], h), cols_of(MATS[i], k)]
+        return rcopy(ref, ref, ag_send.at[i, d, p], ag_recv.at[i, d, p], dev[d])
+
+    def ag_forward(i, d):
+        ref = full[i].at[half_of(MATS[i], d), cols_of(MATS[i], (left, right)[d])]
+        return rcopy(ref, ref, ag_send.at[i, d, 2], ag_recv.at[i, d, 2], dev[d])
 
     me_xy = x * 4 + y
     for i in range(2):
@@ -159,10 +188,14 @@
                 k = h * (mat.tiles // 2) + t
                 at = t if i == 0 else 4
                 q_mine[h, at : at + 1, :] = col[:, k * 128 : (k + 1) * 128]
+        if i == 0:
+            for d in range(2):
+                go(ag_own(i, d, 0))
     for b in range(5):
         block = lanes[b * 128 : (b + 1) * 128, :].T
         rows_buf[me_xy, b : b + 1, :] = jnp.sum(block, axis=0, keepdims=True)
 
+    hear(2)
     def s1(a, b, peer):
         return rcopy(
             rows_buf.at[me_xy if peer is None else peer, pl.ds(0, 5)], rows_buf.at[me_xy if peer is None else peer, pl.ds(0, 5)],
@@ -177,25 +210,9 @@
 
     go(to_core(q_mine, q_sib, 0))
 
-    def ag_own(i, d, p):
-        h = d if p == 0 else 1 - d
-        ref = full[i].at[half_of(MATS[i], h), cols_of(MATS[i], x)]
-        return rcopy(ref, ref, ag_send.at[i, d, p], ag_recv.at[i, d, p], dev[d])
-
-    def ag_landed(i, d, p):
-        h = d if p != 1 else 1 - d
-        k = over if p == 2 else (left, right)[d]
-        ref = full[i].at[half_of(MATS[i], h), cols_of(MATS[i], k)]
-        return rcopy(ref, ref, ag_send.at[i, d, p], ag_recv.at[i, d, p], dev[d])
-
-    def ag_forward(i, d):
-        ref = full[i].at[half_of(MATS[i], d), cols_of(MATS[i], (left, right)[d])]
-        return rcopy(ref, ref, ag_send.at[i, d, 2], ag_recv.at[i, d, 2], dev[d])
-
-    for p in range(2):
-        for i in range(2):
-            for d in range(2):
-                go(ag_own(i, d, p))
+    for i, p in ((1, 0), (0, 1), (1, 1)):
+        for d in range(2):
+            go(ag_own(i, d, p))
 
     def to_z(buf, j, k, peer):
         slot = z if peer is None else peer
@@ -313,7 +330,25 @@
     cf_g[...] = lax.rsqrt(gate_cols_new[...]) * factors[0]
     cf_o[...] = lax.rsqrt(out_cols_new[...]) * factors[1]
 
+    for copy in sends:
+        copy.wait_send()
+
+
+def finish(
+    full_g, full_o, rmat, cf_g, cf_o, gate_r, gate_c, out_r, out_c,
+    gate_up, gate_rows_new, gate_cols_new, out_up, out_rows_new, out_cols_new,
+    res_g, res_o, store_sem,
+):
     stores = []
+
+    def store(src, dst):
+        stores.append(pltpu.make_async_copy(src, dst, store_sem.at[len(stores)]))
+        stores[-1].start()
+
+    store(gate_r, gate_rows_new)
+    store(gate_c, gate_cols_new)
+    store(out_r, out_rows_new)
+    store(out_c, out_cols_new)
     for k in range(4):
 
         def scale(t, _, k=k):
@@ -322,33 +357,71 @@
             return 0
 
         lax.fori_loop(0, 8, scale, 0)
-        part = res_g.at[:, pl.ds(k * 1024, 1024)]
-        stores.append(pltpu.make_async_copy(part, gate_up.at[:, pl.ds(k * 1024, 1024)], store_sem.at[k]))
-        stores[-1].start()
+        part = pl.ds(k * 1024, 1024)
+        store(res_g.at[:, part], gate_up.at[:, part])
     for k in range(4):
 
         def scale(t, _, k=k):
             cols = pl.ds(pl.multiple_of(t * 128, 128), 128)
             rows = pl.ds(k * 128, 128)
-            res_o[rows, cols] = (full_o[rows, cols].astype(F32) * rmat[(k + 1) * 128 : (k + 2) * 128, :] * cf_o[pl.ds(t, 1), :]).astype(BF16)
+            by_row = rmat[(k + 1) * 128 : (k + 2) * 128, :]
+            res_o[rows, cols] = (full_o[rows, cols].astype(F32) * by_row * cf_o[pl.ds(t, 1), :]).astype(BF16)
             return 0
 
         lax.fori_loop(0, 8, scale, 0)
-        part = res_o.at[pl.ds(k * 128, 128)]
-        stores.append(pltpu.make_async_copy(part, out_up.at[pl.ds(k * 128, 128)], store_sem.at[4 + k]))
-        stores[-1].start()
-    for copy in sends:
-        copy.wait_send()
-    for store in stores:
-        store.wait()
+        part = pl.ds(k * 128, 128)
+        store(res_o.at[part], out_up.at[part])
+    for copy in stores:
+        copy.wait()
 
 
 def local(zs, gate_grads, gate_rows, gate_cols, out_grads, out_rows, out_cols):
-    vmem, hbm = pl.BlockSpec(memory_space=pltpu.VMEM), pl.BlockSpec(memory_space=pl.ANY)
+    vmem, hbm = pl.BlockSpec(memory_space=pltpu.VMEM), pl.BlockSpec(memory_space=pltpu.HBM)
     dma, buf = pltpu.SemaphoreType.DMA, pltpu.VMEM
     tile = (8, 128)
+    held = pl.pallas_call(
+        functools.partial(kernel, zs),
+        out_shape=(
+            jax.ShapeDtypeStruct((128, 4096), BF16),
+            jax.ShapeDtypeStruct((512, 1024), BF16),
+            jax.ShapeDtypeStruct((640, 128), F32),
+            jax.ShapeDtypeStruct((32, 128), F32),
+            jax.ShapeDtypeStruct((8, 128), F32),
+            jax.ShapeDtypeStruct((1, 128), F32),
+            jax.ShapeDtypeStruct((32, 128), F32),
+            jax.ShapeDtypeStruct((4, 128), F32),
+            jax.ShapeDtypeStruct((8, 128), F32),
+        ),
+        in_specs=[hbm] * 6,
+        out_specs=(vmem,) * 9,
+        scratch_shapes=[
+            buf((1, 128), F32), buf((32, 128), F32), buf((4, 128), F32), buf((8, 128), F32),
+            buf((128, 4096), BF16), buf((512, 1024), BF16),
+            buf((2, 64, 1024), BF16), buf((2, 256, 256), BF16),
+            buf((2, 64, 1024), BF16), buf((2, 256, 256), BF16),
+            buf((2, 128, 1024), BF16), buf((2, 512, 256), BF16),
+            buf((128, 1024), F32), buf((512, 256), F32),
+            buf((640, 128), F32),
+            buf((16, *tile), F32),
+            buf((2, *tile), F32), buf(tile, F32), buf((zs, *tile), F32),
+            buf((2, *tile), F32), buf(tile, F32), buf((zs, *tile), F32),
+            buf((32, *tile), F32),
+            pltpu.SemaphoreType.REGULAR((3,)),
+            dma((6,)), dma((2, 2, 3)), dma((2, 2, 3)), dma((2, 2, 3)), dma((2, 2, 3)),
+            dma((16,)), dma((16,)), dma((2,)), dma((2,)), dma((2, zs)), dma((2, zs)), dma((32,)), dma((32,)),
+        ],
+        compiler_params=pltpu.CompilerParams(collective_id=0, has_side_effects=True, vmem_limit_bytes=32 << 20),
+    )(
+        *(
+            pltpu.with_memory_space_constraint(a, pltpu.HBM)
+            for a in (
+                gate_grads, gate_rows.reshape(1, 128), gate_cols.reshape(32, 128),
+                out_grads, out_rows.reshape(4, 128), out_cols.reshape(8, 128),
+            )
+        )
+    )
     outs = pl.pallas_call(
-        functools.partial(kernel, zs),
+        finish,
         out_shape=(
             jax.ShapeDtypeStruct((128, 4096), BF16),
             jax.ShapeDtypeStruct((1, 128), F32),
@@ -357,29 +430,11 @@
             jax.ShapeDtypeStruct((4, 128), F32),
             jax.ShapeDtypeStruct((8, 128), F32),
         ),
-        in_specs=[hbm, vmem, vmem, hbm, vmem, vmem],
-        out_specs=(hbm, vmem, vmem, hbm, vmem, vmem),
-        scratch_shapes=[
-            buf((128, 4096), BF16), buf((512, 1024), BF16),
-            buf((2, 64, 1024), BF16), buf((2, 256, 256), BF16),
-            buf((2, 64, 1024), BF16), buf((2, 256, 256), BF16),
-            buf((2, 128, 1024), BF16), buf((2, 512, 256), BF16),
-            buf((128, 4096), BF16), buf((512, 1024), BF16),
-            buf((128, 4096), BF16), buf((512, 1024), BF16),
-            buf((128, 1024), F32), buf((512, 256), F32),
-            buf((640, 128), F32), buf((640, 128), F32),
-            buf((16, *tile), F32),
-            buf((2, *tile), F32), buf(tile, F32), buf((zs, *tile), F32),
-            buf((2, *tile), F32), buf(tile, F32), buf((zs, *tile), F32),
-            buf((32, *tile), F32), buf((32, 128), F32), buf(tile, F32),
-            dma((2,)), dma((8,)), dma((2, 2, 3)), dma((2, 2, 3)), dma((2, 2, 3)), dma((2, 2, 3)),
-            dma((16,)), dma((16,)), dma((2,)), dma((2,)), dma((2, zs)), dma((2, zs)), dma((32,)), dma((32,)),
-        ],
-        compiler_params=pltpu.CompilerParams(collective_id=0, has_side_effects=True, vmem_limit_bytes=48 << 20),
-    )(
-        gate_grads, gate_rows.reshape(1, 128), gate_cols.reshape(32, 128),
-        out_grads, out_rows.reshape(4, 128), out_cols.reshape(8, 128),
-    )
+        in_specs=[vmem] * 9,
+        out_specs=(hbm,) * 6,
+        scratch_shapes=[buf((128, 4096), BF16), buf((512, 1024), BF16), dma((12,))],
+        compiler_params=pltpu.CompilerParams(vmem_limit_bytes=32 << 20),
+    )(*held)
     gate_up, gate_r, gate_c, out_up, out_r, out_c = outs
     return gate_up, gate_r.reshape(128), gate_c.reshape(4096), out_up, out_r.reshape(512), out_c.reshape(1024)
 

time: 71.7 us -> 59.4 us (0.83)
  local copies, waits for them, and re-layouts: 8.07 us -> 0 us
  Pallas kernels: 62.6 us -> 58.6 us
    unnamed x18 -> x0, local copies, waits for them, and re-layouts: 8.07 us -> none
    pallas_call x1, Pallas kernels: 62.6 us -> 56.7 us  [local(): pl.pallas_call(functools.partial(kernel, zs), out_shape=(jax.ShapeDtypeSt...]
    pallas_call x0 -> x1, Pallas kernels: none -> 1.88 us  [local(): pl.pallas_call(finish, out_shape=(jax.ShapeDtypeStruct((128, 4096), BF16)...]
where the time goes in v2:
time: 59.4 us; the launch traced here: 59.2 us
  Pallas kernels  58.6 us (99%)
  between operations  0.64 us (1%)
    pallas_call x1, Pallas kernels, local(): pl.pallas_call(functools.partial(kernel, zs), out_shape=(jax.ShapeDtypeSt...  56.7 us
    pallas_call x1, Pallas kernels, local(): pl.pallas_call(finish, out_shape=(jax.ShapeDtypeStruct((128, 4096), BF16)...  1.88 us

profile of v2, /device:TPU:1, one launch (start us, length us, event | category | flops | bytes accessed | tf_op | source)
XLA Modules:
  0.0 59.2 jit_solution(15928993899267515491)
XLA Ops:
  0.6 56.7 %shard_map.109 = (bf16[128,4096]{1,0:T(8,128)(2,1)S(1)}, bf16[512,1024]{1,0:T(8,128)(2,1)S(1)}, f32[640,128]{1,0:T(8,128)S(1)}, f32[32,128]{1,0:T(8,128)S(1)}, f...) custom-call(bf16[1,128,4096]{2,1,0:T(8,128)(2,1)} %gate_in.1, ...), custom_call_target="tpu_custom_call" | custom-call | tf_op jit(solution)/shard_map/pallas_call | solution.py:382
  57.3 1.9 %shard_map.110 = (bf16[128,4096]{1,0:T(8,128)(2,1)}, f32[1,128]{1,0:T(1,128)}, f32[32,128]{1,0:T(8,128)}, bf16[512,1024]{1,0:T(8,128)(2,1)}, f32[4,128]{1,0:T(4,128)}, /*index=5*/f32[8,128]{1,0:T(8,128)}) custom-call(bf16[128,4096]{1,0:T(8,128)(2,1)S(1)} %get-tuple-element.21.full_g, bf16[512,1024]{1,0:T(8,128)(2,1)S(1)} %get-tuple-element.22.full_o, ...), custom_call_target="tpu_custom_call" | custom-call | tf_op jit(solution)/shard_map/pallas_call | solution.py:423

commit v3 on v2

--- a/solution.py
+++ b/solution.py
@@ -22,6 +22,7 @@
         self.chunk = width // 4
         self.half = rows // 2
         self.tiles = self.chunk // 128
+        self.parts = max(1, self.half // 128)
 
 
 GATE = Mat(128, 4096, D, FF, 0)
@@ -49,17 +50,36 @@
     full_g, full_o, rmat, cf_g, cf_o, gate_rows_new, gate_cols_new, out_rows_new, out_cols_new,
     gate_rows, gate_cols, out_rows, out_cols,
     own_g, own_o, tr_g, tr_o, st_g, st_o, fr_g, fr_o,
-    sq_g, sq_o, lanes, rows_buf, q_mine, q_sib, q_z, w_mine, w_sib, w_z, e_buf,
+    sq_g, sq_o, lanes, rows_buf, q_mine, q_sib, q_z, w_mine, w_sib, w_z, c_buf, e_buf,
     token, load_sem, rs_send, rs_recv, ag_send, ag_recv,
-    s1_send, s1_recv, core_send, core_recv, z_send, z_recv, s3_send, s3_recv,
+    s1_send, s1_recv, core_send, core_recv, z_send, z_recv, s2_send, s2_recv, s3_send, s3_recv,
 ):
     x, r, y = lax.axis_index("dp"), lax.axis_index("row"), lax.axis_index("col")
     z, core = r // 2, r % 2
     right, left, over = (x + 1) % 4, (x + 3) % 4, (x + 2) % 4
     dev = ((right, r, y), (left, r, y))
     sibling = (x, z * 2 + (1 - core), y)
-    own, tr, st, fr, full = (own_g, own_o), (tr_g, tr_o), (st_g, st_o), (fr_g, fr_o), (full_g, full_o)
-
+    ins, own, tr, st, fr, full = (gate_in, out_in), (own_g, own_o), (tr_g, tr_o), (st_g, st_o), (fr_g, fr_o), (full_g, full_o)
+
+    hops = lambda k, n: min(k, n - k)
+    far = sorted(((i, j) for i in range(4) for j in range(4) if i or j), key=lambda p: -hops(p[0], 4) - hops(p[1], 4))
+    xy_partners = [((x + i) % 4, (y + j) % 4) for i, j in far]
+    z_partners = [(z + k) % zs for k in sorted(range(1, zs), key=lambda k: -hops(k, zs))]
+    along_z = lambda k: (x, ((z + k + zs) % zs) * 2 + core, y)
+    across_x, across_y = (over, r, y), (x, r, (y + 2) % 4)
+    nearest = [dev[0], dev[1], (x, r, (y + 1) % 4), (x, r, (y + 3) % 4), along_z(1), along_z(-1), sibling]
+    rounds = (nearest, [across_x, across_y, along_z(2), along_z(-2), sibling], [along_z(4), along_z(-4), across_x])
+
+    def tell(k):
+        for who in rounds[k]:
+            pl.semaphore_signal(token.at[k], inc=1, device_id=who, device_id_type=MESH)
+
+    def hear(k):
+        pl.semaphore_wait(token.at[k], len(rounds[k]))
+
+    barrier = pltpu.get_barrier_semaphore()
+    for who in nearest:
+        pl.semaphore_signal(barrier, inc=1, device_id=who, device_id_type=MESH)
     loads = [
         pltpu.make_async_copy(src, dst, load_sem.at[i])
         for i, (src, dst) in enumerate(
@@ -72,27 +92,8 @@
     for load in loads:
         load.start()
 
-    xy_partners = [((x + i) % 4, (y + j) % 4) for i in range(4) for j in range(4) if i or j]
-    z_partners = [(z + k) % zs for k in range(1, zs)]
-    along_z = lambda k: (x, ((z + k + zs) % zs) * 2 + core, y)
-    across_x, across_y = (over, r, y), (x, r, (y + 2) % 4)
-    nearest = [dev[0], dev[1], (x, r, (y + 1) % 4), (x, r, (y + 3) % 4), along_z(1), along_z(-1), sibling]
-    rounds = (nearest, [across_x, across_y, along_z(2), along_z(-2), sibling], [along_z(4), along_z(-4), across_x])
-
-    def tell(k):
-        for who in rounds[k]:
-            pl.semaphore_signal(token.at[k], inc=1, device_id=who, device_id_type=MESH)
-
-    def hear(k):
-        pl.semaphore_wait(token.at[k], len(rounds[k]))
-
-    barrier = pltpu.get_barrier_semaphore()
-    for who in nearest:
-        pl.semaphore_signal(barrier, inc=1, device_id=who, device_id_type=MESH)
     q_mine[...] = jnp.zeros_like(q_mine)
     w_mine[...] = jnp.zeros_like(w_mine)
-    for load in loads:
-        load.wait()
     pl.semaphore_wait(barrier, len(nearest))
 
     sends = []
@@ -103,21 +104,22 @@
 
     def rs_transit(i, d):
         return rcopy(
-            own[i].at[half_of(MATS[i], d), cols_of(MATS[i], over)], tr[i].at[d],
+            ins[i].at[0, half_of(MATS[i], d), cols_of(MATS[i], over)], tr[i].at[d],
             rs_send.at[i, d, 0], rs_recv.at[i, d, 0], dev[d],
         )
 
     def rs_alone(i, d):
         to = (right, left)[d]
         return rcopy(
-            own[i].at[half_of(MATS[i], 1 - d), cols_of(MATS[i], to)], fr[i].at[d, half_of(MATS[i], 1 - d)],
+            ins[i].at[0, half_of(MATS[i], 1 - d), cols_of(MATS[i], to)], fr[i].at[d, half_of(MATS[i], 1 - d)],
             rs_send.at[i, d, 1], rs_recv.at[i, d, 1], dev[d],
         )
 
-    def rs_sum(i, d):
+    def rs_sum(i, d, p):
+        size = MATS[i].half // MATS[i].parts
         return rcopy(
-            st[i].at[d], fr[i].at[d, half_of(MATS[i], d)],
-            rs_send.at[i, d, 2], rs_recv.at[i, d, 2], dev[d],
+            st[i].at[d, pl.ds(p * size, size)], fr[i].at[d, pl.ds(d * MATS[i].half + p * size, size)],
+            rs_send.at[i, d, 2 + p], rs_recv.at[i, d, 2 + p], dev[d],
         )
 
     for make in (rs_transit, rs_alone):
@@ -125,6 +127,8 @@
             for d in range(2):
                 go(make(i, d))
     tell(0)
+    for load in loads:
+        load.wait()
     for i in range(2):
         mat = MATS[i]
         for d in range(2):
@@ -139,7 +143,8 @@
                 return 0
 
             lax.fori_loop(0, mat.half // step, add, 0)
-            go(rs_sum(i, d))
+            for p in range(mat.parts):
+                go(rs_sum(i, d, p))
         hear(i)
         tell(i + 1)
 
@@ -164,11 +169,10 @@
         sq = (sq_g, sq_o)[i]
         for d in range(2):
             rs_alone(i, d).wait_recv()
-            rs_sum(i, d).wait_recv()
         step = 16384 // mat.chunk
 
         def total(n, acc, i=i, mat=mat, sq=sq, step=step):
-            rows = pl.ds(pl.multiple_of(n * step, 16), step)
+            rows = pl.ds(n * step, step)
             s = own[i][rows, cols_of(mat, x)].astype(F32) + fr[i][0, rows, :].astype(F32) + fr[i][1, rows, :].astype(F32)
             full[i][rows, cols_of(mat, x)] = s.astype(BF16)
             s = s * s
@@ -176,24 +180,33 @@
             by_lane = s[:, 0:128]
             for t in range(1, mat.tiles):
                 by_lane = by_lane + s[:, t * 128 : (t + 1) * 128]
-            lanes[pl.ds(pl.multiple_of(mat.first_row + n * step, 8), step), :] = by_lane
+            lanes[pl.ds(mat.first_row + n * step, step), :] = by_lane
             for k in range(step // 8):
                 acc = acc + s[k * 8 : (k + 1) * 8, :]
             return acc
 
-        acc = lax.fori_loop(0, mat.rows // step, total, jnp.zeros((8, mat.chunk), F32))
+        acc = jnp.zeros((8, mat.chunk), F32)
+        size = mat.half // mat.parts
+        for p in range(mat.parts):
+            for d in range(2):
+                rs_sum(i, d, p).wait_recv()
+            for d in range(2):
+                first = d * mat.half + p * size
+                for n in range(first // step, (first + size) // step):
+                    acc = total(n, acc)
+                if mat.parts > 1 or d == 1:
+                    b = (mat.first_row + first) // 128
+                    block = lanes[b * 128 : (b + 1) * 128, :].T
+                    rows_buf[me_xy, b : b + 1, :] = jnp.sum(block, axis=0, keepdims=True)
+        if i == 0:
+            for d in range(2):
+                go(ag_own(i, d, 0))
         col = jnp.sum(acc, axis=0, keepdims=True)
         for h in range(2):
             for t in range(mat.tiles // 2):
                 k = h * (mat.tiles // 2) + t
                 at = t if i == 0 else 4
                 q_mine[h, at : at + 1, :] = col[:, k * 128 : (k + 1) * 128]
-        if i == 0:
-            for d in range(2):
-                go(ag_own(i, d, 0))
-    for b in range(5):
-        block = lanes[b * 128 : (b + 1) * 128, :].T
-        rows_buf[me_xy, b : b + 1, :] = jnp.sum(block, axis=0, keepdims=True)
 
     hear(2)
     def s1(a, b, peer):
@@ -208,16 +221,18 @@
     def to_core(buf, got, j):
         return rcopy(buf.at[1 - core], got, core_send.at[j], core_recv.at[j], sibling)
 
-    go(to_core(q_mine, q_sib, 0))
 
     for i, p in ((1, 0), (0, 1), (1, 1)):
         for d in range(2):
             go(ag_own(i, d, p))
+        if (i, p) == (1, 0):
+            go(to_core(q_mine, q_sib, 0))
 
     def to_z(buf, j, k, peer):
         slot = z if peer is None else peer
+        rows = pl.ds(0, (5, 16)[j])
         return rcopy(
-            buf.at[slot], buf.at[slot], z_send.at[j, k], z_recv.at[j, slot], (x, k * 2 + core, y)
+            buf.at[slot, rows], buf.at[slot, rows], z_send.at[j, k], z_recv.at[j, slot], (x, k * 2 + core, y)
         )
 
     to_core(q_mine, q_sib, 0).wait_recv()
@@ -225,7 +240,7 @@
     for k in z_partners:
         go(to_z(q_z, 0, k, None))
 
-    for a, b in xy_partners:
+    for a, b in xy_partners[::-1]:
         s1(a, b, a * 4 + b).wait_recv()
     row_sum = rows_buf[0, 0:5, :]
     for k in range(1, 16):
@@ -256,25 +271,27 @@
             return tuple(out)
 
         acc = lax.fori_loop(0, mat.rows // step, weigh, tuple(jnp.zeros((8, 128), F32) for _ in range(mat.tiles)))
-        for h in range(2):
-            for t in range(mat.tiles // 2):
-                at = t if i == 0 else 4
-                w_mine[h, at : at + 1, :] = jnp.sum(acc[h * (mat.tiles // 2) + t], axis=0, keepdims=True)
-    for h in range(2):
-        w_mine[h, 5:6, :] = g_rows
-        w_mine[h, 6:7, :] = jnp.sum(o_rows, axis=0, keepdims=True)
-    go(to_core(w_mine, w_sib, 1))
-    to_core(w_mine, w_sib, 1).wait_recv()
-    w_z[z] = w_mine[core] + w_sib[...]
+        for t in range(mat.tiles):
+            at = t if i == 0 else 8 + t
+            w_mine[at : at + 1, :] = jnp.sum(acc[t], axis=0, keepdims=True)
+    for at in (10, 12):
+        w_mine[at : at + 1, :] = g_rows
+        w_mine[at + 1 : at + 2, :] = jnp.sum(o_rows, axis=0, keepdims=True)
+    w_pair = rcopy(w_mine, w_sib, core_send.at[1], core_recv.at[1], sibling)
+    go(w_pair)
+    w_pair.wait_recv()
+    w = w_mine[...] + w_sib[...]
+    w = jnp.where(lax.broadcasted_iota(jnp.int32, w.shape, 0) >= 12, w - w.astype(BF16).astype(F32), w)
+    w_z[z] = w.astype(BF16)
     for k in z_partners:
         go(to_z(w_z, 1, k, None))
 
-    for i in range(2):
+    for i in (0,):
         for d in range(2):
             ag_landed(i, d, 0).wait_recv()
             go(ag_forward(i, d))
 
-    for k in z_partners:
+    for k in z_partners[::-1]:
         to_z(q_z, 0, k, k).wait_recv()
     q = q_z[0]
     for k in range(1, zs):
@@ -283,55 +300,69 @@
     old_o = out_cols[pl.ds(x * 2 + core, 1), :]
     c_g = KEEP * old_g + (1.0 - KEEP) * (q[0:4] * (1.0 / D) + TINY)
     c_o = KEEP * old_o + (1.0 - KEEP) * (q[4:5] * (1.0 / FF) + TINY)
-    for k in z_partners:
+    me_c = x * 2 + core
+    c_buf[me_c, 0:4, :] = c_g
+    c_buf[me_c, 4:5, :] = c_o
+
+    def s2(a, h, peer):
+        slot = me_c if peer is None else peer
+        part = c_buf.at[slot, pl.ds(0, 5)]
+        return rcopy(part, part, s2_send.at[a * 2 + h], s2_recv.at[slot], (a, z * 2 + h, y))
+
+    c_partners = [(over, 1 - core), (over, core), (right, 1 - core), (left, 1 - core), (right, core), (left, core), (x, 1 - core)]
+    for a, h in c_partners:
+        go(s2(a, h, None))
+    for i in (1,):
+        for d in range(2):
+            ag_landed(i, d, 0).wait_recv()
+            go(ag_forward(i, d))
+
+    s2(x, 1 - core, x * 2 + 1 - core).wait_recv()
+    inv = [1.0 / c_buf[x * 2 + h, 0:5, :] for h in range(2)]
+    for k in z_partners[::-1]:
         to_z(w_z, 1, k, k).wait_recv()
-    w = w_z[0]
+    w = w_z[0].astype(F32)
     for k in range(1, zs):
-        w = w + w_z[k]
-    me_e = (x * 4 + y) * 2 + core
-    e_buf[me_e, 0:4, :] = c_g
-    e_buf[me_e, 4:5, :] = c_o
-    e_buf[me_e, 5:6, :] = jnp.sum(w[0:4] / c_g, axis=0, keepdims=True)
-    e_buf[me_e, 6:7, :] = w[4:5] / c_o
-    e_buf[me_e, 7:8, :] = jnp.zeros((1, 128), F32)
-
-    def s3(a, b, h, peer):
-        slot = me_e if peer is None else peer
-        return rcopy(
-            e_buf.at[slot], e_buf.at[slot], s3_send.at[(a * 4 + b) * 2 + h], s3_recv.at[slot], (a, z * 2 + h, b)
-        )
-
-    e_partners = [(x, y, 1 - core)] + [(a, b, h) for a, b in xy_partners for h in (core, 1 - core)]
-    for a, b, h in e_partners:
-        go(s3(a, b, h, None))
-
-    row_total = (jnp.sum(w[5:6]), jnp.sum(w[6:7]))
+        w = w + w_z[k].astype(F32)
+
+    e_buf[me_xy, 0:1, :] = jnp.sum(w[0:4] * inv[0][0:4] + w[4:8] * inv[1][0:4], axis=0, keepdims=True)
+    e_buf[me_xy, 1:2, :] = w[8:9] * inv[0][4:5] + w[9:10] * inv[1][4:5]
+
+    def s3(a, b, peer):
+        slot = me_xy if peer is None else peer
+        part = e_buf.at[slot, pl.ds(0, 2)]
+        return rcopy(part, part, s3_send.at[a * 4 + b], s3_recv.at[slot], (a, r, b))
+
+    for a, b in xy_partners:
+        go(s3(a, b, None))
+
+    means = [jnp.sum(w[10 + i : 11 + i] + w[12 + i : 13 + i], axis=1, keepdims=True) * (1.0 / MATS[i].m) for i in range(2)]
+    for a, h in c_partners[-2::-1]:
+        s2(a, h, a * 2 + h).wait_recv()
+    for k in range(4):
+        for h in range(2):
+            slot = k * 2 + h
+            gate_cols_new[8 * k + 4 * h : 8 * k + 4 * h + 4, :] = c_buf[slot, 0:4, :]
+            out_cols_new[2 * k + h : 2 * k + h + 1, :] = c_buf[slot, 4:5, :]
+    cf_g[...] = lax.rsqrt(gate_cols_new[...])
+    cf_o[...] = lax.rsqrt(out_cols_new[...])
     for i in range(2):
         for d in range(2):
             for p in (1, 2):
                 ag_landed(i, d, p).wait_recv()
-    for a, b, h in e_partners:
-        s3(a, b, h, (a * 4 + b) * 2 + h).wait_recv()
-    e = e_buf[0, 5:7, :]
-    for k in range(1, 32):
-        e = e + e_buf[k, 5:7, :]
-    factors = []
-    for i in range(2):
-        mean = row_total[i] * (1.0 / MATS[i].m)
-        energy = jnp.sum(e[i : i + 1])
-        mean = jnp.full((1, 128), mean, F32)
-        root = jnp.sqrt(mean * (energy * (1.0 / (D * FF))))
-        factors.append(jnp.sqrt(mean) / jnp.maximum(1.0, root))
-    for k in range(4):
-        for h in range(2):
-            slot = (k * 4 + y) * 2 + h
-            gate_cols_new[8 * k + 4 * h : 8 * k + 4 * h + 4, :] = e_buf[slot, 0:4, :]
-            out_cols_new[2 * k + h : 2 * k + h + 1, :] = e_buf[slot, 4:5, :]
-    cf_g[...] = lax.rsqrt(gate_cols_new[...]) * factors[0]
-    cf_o[...] = lax.rsqrt(out_cols_new[...]) * factors[1]
-
     for copy in sends:
         copy.wait_send()
+    for a, b in xy_partners[::-1]:
+        s3(a, b, a * 4 + b).wait_recv()
+    e = e_buf[0, 0:2, :]
+    for k in range(1, 16):
+        e = e + e_buf[k, 0:2, :]
+    for i in range(2):
+        energy = jnp.sum(e[i : i + 1], axis=1, keepdims=True)
+        root = jnp.sqrt(means[i] * (energy * (1.0 / (D * FF))))
+        factor = jnp.sqrt(means[i]) / jnp.maximum(1.0, root)
+        cf = (cf_g, cf_o)[i]
+        cf[...] = cf[...] * factor
 
 
 def finish(
@@ -356,7 +387,7 @@
             res_g[:, cols] = (full_g[:, cols].astype(F32) * rmat[0:128, :] * cf_g[pl.ds(k * 8 + t, 1), :]).astype(BF16)
             return 0
 
-        lax.fori_loop(0, 8, scale, 0)
+        lax.fori_loop(0, 8, scale, 0, unroll=True)
         part = pl.ds(k * 1024, 1024)
         store(res_g.at[:, part], gate_up.at[:, part])
     for k in range(4):
@@ -368,7 +399,7 @@
             res_o[rows, cols] = (full_o[rows, cols].astype(F32) * by_row * cf_o[pl.ds(t, 1), :]).astype(BF16)
             return 0
 
-        lax.fori_loop(0, 8, scale, 0)
+        lax.fori_loop(0, 8, scale, 0, unroll=True)
         part = pl.ds(k * 128, 128)
         store(res_o.at[part], out_up.at[part])
     for copy in stores:
@@ -404,11 +435,11 @@
             buf((640, 128), F32),
             buf((16, *tile), F32),
             buf((2, *tile), F32), buf(tile, F32), buf((zs, *tile), F32),
-            buf((2, *tile), F32), buf(tile, F32), buf((zs, *tile), F32),
-            buf((32, *tile), F32),
+            buf((16, 128), F32), buf((16, 128), F32), buf((zs, 16, 128), BF16),
+            buf((8, *tile), F32), buf((16, *tile), F32),
             pltpu.SemaphoreType.REGULAR((3,)),
-            dma((6,)), dma((2, 2, 3)), dma((2, 2, 3)), dma((2, 2, 3)), dma((2, 2, 3)),
-            dma((16,)), dma((16,)), dma((2,)), dma((2,)), dma((2, zs)), dma((2, zs)), dma((32,)), dma((32,)),
+            dma((6,)), dma((2, 2, 4)), dma((2, 2, 4)), dma((2, 2, 3)), dma((2, 2, 3)),
+            dma((16,)), dma((16,)), dma((2,)), dma((2,)), dma((2, zs)), dma((2, zs)), dma((8,)), dma((8,)), dma((16,)), dma((16,)),
         ],
         compiler_params=pltpu.CompilerParams(collective_id=0, has_side_effects=True, vmem_limit_bytes=32 << 20),
     )(

time: 59.4 us -> 55.4 us (0.933)
  Pallas kernels: 58.6 us -> 54.7 us
    pallas_call x1, Pallas kernels: 56.7 us -> 53.2 us  [local(): pl.pallas_call(functools.partial(kernel, zs), out_shape=(jax.ShapeDtypeSt...]
where the time goes in v3:
time: 55.4 us; the launch traced here: 55.3 us
  Pallas kernels  54.7 us (99%)
  between operations  0.64 us (1%)
    pallas_call x1, Pallas kernels, local(): pl.pallas_call(functools.partial(kernel, zs), out_shape=(jax.ShapeDtypeSt...  53.2 us
    pallas_call x1, Pallas kernels, local(): pl.pallas_call(finish, out_shape=(jax.ShapeDtypeStruct((128, 4096), BF16)...  1.49 us

profile of v3, /device:TPU:1, one launch (start us, length us, event | category | flops | bytes accessed | tf_op | source)
XLA Modules:
  0.0 55.3 jit_solution(6919447167022028110)
XLA Ops:
  0.6 53.2 %shard_map.109 = (bf16[128,4096]{1,0:T(8,128)(2,1)S(1)}, bf16[512,1024]{1,0:T(8,128)(2,1)S(1)}, f32[640,128]{1,0:T(8,128)S(1)}, f32[32,128]{1,0:T(8,128)S(1)}, f...) custom-call(bf16[1,128,4096]{2,1,0:T(8,128)(2,1)} %gate_in.1, ...), custom_call_target="tpu_custom_call" | custom-call | tf_op jit(solution)/shard_map/pallas_call | solution.py:413
  53.8 1.5 %shard_map.110 = (bf16[128,4096]{1,0:T(8,128)(2,1)}, f32[1,128]{1,0:T(1,128)}, f32[32,128]{1,0:T(8,128)}, bf16[512,1024]{1,0:T(8,128)(2,1)}, f32[4,128]{1,0:T(4,128)}, /*index=5*/f32[8,128]{1,0:T(8,128)}) custom-call(bf16[128,4096]{1,0:T(8,128)(2,1)S(1)} %get-tuple-element.21.full_g, bf16[512,1024]{1,0:T(8,128)(2,1)S(1)} %get-tuple-element.22.full_o, ...), custom_call_target="tpu_custom_call" | custom-call | tf_op jit(solution)/shard_map/pallas_call | solution.py:454

commit v4 on v3

--- a/solution.py
+++ b/solution.py
@@ -296,8 +296,10 @@
     q = q_z[0]
     for k in range(1, zs):
         q = q + q_z[k]
-    old_g = gate_cols[pl.ds(pl.multiple_of(x * 8 + core * 4, 4), 4), :]
-    old_o = out_cols[pl.ds(x * 2 + core, 1), :]
+    old_g = gate_cols[pl.ds(pl.multiple_of(x * 8, 8), 8), :]
+    old_g = jnp.where(core == 0, old_g[0:4], old_g[4:8])
+    mine = lax.broadcasted_iota(jnp.int32, (8, 128), 0) == x * 2 + core
+    old_o = jnp.sum(jnp.where(mine, out_cols[...], 0.0), axis=0, keepdims=True)
     c_g = KEEP * old_g + (1.0 - KEEP) * (q[0:4] * (1.0 / D) + TINY)
     c_o = KEEP * old_o + (1.0 - KEEP) * (q[4:5] * (1.0 / FF) + TINY)
     me_c = x * 2 + core

time: 55.4 us -> 55.4 us (level)
  no operation moved by 1% of the time
where the time goes in v4:
time: 55.4 us; the launch traced here: 55.3 us
  Pallas kernels  54.7 us (99%)
  between operations  0.64 us (1%)
    pallas_call x1, Pallas kernels, local(): pl.pallas_call(functools.partial(kernel, zs), out_shape=(jax.ShapeDtypeSt...  53.2 us
    pallas_call x1, Pallas kernels, local(): pl.pallas_call(finish, out_shape=(jax.ShapeDtypeStruct((128, 4096), BF16)...  1.49 us

profile of v4, /device:TPU:1, one launch (start us, length us, event | category | flops | bytes accessed | tf_op | source)
XLA Modules:
  0.0 55.3 jit_solution(9637840940823093956)
XLA Ops:
  0.6 53.2 %shard_map.109 = (bf16[128,4096]{1,0:T(8,128)(2,1)S(1)}, bf16[512,1024]{1,0:T(8,128)(2,1)S(1)}, f32[640,128]{1,0:T(8,128)S(1)}, f32[32,128]{1,0:T(8,128)S(1)}, f...) custom-call(bf16[1,128,4096]{2,1,0:T(8,128)(2,1)} %gate_in.1, ...), custom_call_target="tpu_custom_call" | custom-call | tf_op jit(solution)/shard_map/pallas_call | solution.py:415
  53.8 1.5 %shard_map.110 = (bf16[128,4096]{1,0:T(8,128)(2,1)}, f32[1,128]{1,0:T(1,128)}, f32[32,128]{1,0:T(8,128)}, bf16[512,1024]{1,0:T(8,128)(2,1)}, f32[4,128]{1,0:T(4,128)}, /*index=5*/f32[8,128]{1,0:T(8,128)}) custom-call(bf16[128,4096]{1,0:T(8,128)(2,1)S(1)} %get-tuple-element.21.full_g, bf16[512,1024]{1,0:T(8,128)(2,1)S(1)} %get-tuple-element.22.full_o, ...), custom_call_target="tpu_custom_call" | custom-call | tf_op jit(solution)/shard_map/pallas_call | solution.py:456
